TPU v7x, 256 devices: a whole 4x4x8 slice. The times are simulated.
256 devices in a mesh: sect: 4 (over z_hi), ctx: 8 (over z_lo, y), tp: 8 (over x, core).
Axes of the slice: x: 4, y: 4, z: 8 (z_hi: 4, z_lo: 2; z = z_hi * 2 + z_lo), core: 2. Of those that a mesh axis runs over, the one named last changes fastest.
Arguments:
- patches: bfloat16 [4096, 1280], P(('sect', 'ctx')), may hold values from -6 to 6
- patch_gain: float32 [1280], replicated, may hold values from 0.25 to 1.75
- patch_shift: float32 [1280], replicated, may hold values from -3 to 3
- encoder_up: bfloat16 [1280, 5120], P(None, 'tp'), may hold values from -0.15625 to 0.15625
- encoder_down: bfloat16 [5120, 1280], P('tp'), may hold values from -0.078125 to 0.078125
- proj_weight: bfloat16 [1280, 8192], P(None, 'tp'), may hold values from -0.15625 to 0.15625
- hidden_text: bfloat16 [8192, 8192], P(('sect', 'ctx'), 'tp'), may hold values from -180 to 180
- slot_source: int32 [64], P(('sect', 'ctx')), may hold values from 0 to 4, as said below
- norm_gain: float32 [8192], P('tp'), may hold values from 0.25 to 1.75
- kv_weight: bfloat16 [2048, 8192], P(None, 'tp'), may hold values from -0.0625 to 0.0625
- queries: bfloat16 [8192, 4096], P(('sect', 'ctx'), 'tp'), may hold values from -40 to 40
Outputs:
- attended: bfloat16 [8192, 4096], P(('sect', 'ctx'), 'tp')
Inputs may be any that keep to these rules, and one draw needn't show every extreme that they name: `slot_source`: for each ctx index, the slots of the blocks with that index carry each value 0 to 3 exactly once, all other slots 4.
All inputs are finite; a program needn't handle non-finite values.
Results may differ from a plain program's by a relative error of at most 0.019.
Values may be sent and summed in bfloat16 or wider, within the bound.
No kernel may reach another device: no remote copies, remote signals or barrier semaphores. Data moves between devices by JAX's collectives and lax.ppermute only.
A program may use at most 128 MiB of HBM per device.

v0:
```python
from functools import partial
import math
import jax
import jax.numpy as jnp
from jax import lax
from jax.sharding import PartitionSpec as P

D = 8192
HEAD = 128
Q_HEADS = 32
KV_HEADS = 8
PATCHES = 128


def layer_norm(values, norm_scale, norm_shift):
    widened = values.astype(jnp.float32)
    center = jnp.mean(widened, axis=-1, keepdims=True)
    spread = jnp.mean(jnp.square(widened - center), axis=-1, keepdims=True)
    return ((widened - center) * lax.rsqrt(spread + 1e-06) * norm_scale + norm_shift).astype(
        jnp.bfloat16
    )


def rotate_keys(keys_in, positions):
    half_size = keys_in.shape[-2] // 2
    frequencies = jnp.exp(
        jnp.arange(half_size, dtype=jnp.float32) * (-2.0 * math.log(500000.0) / (2 * half_size))
    )
    angles = positions[None, :] * frequencies[:, None]
    cosine_table = jnp.cos(angles)
    sine_table = jnp.sin(angles)
    first_half = keys_in[..., :half_size, :]
    second_half = keys_in[..., half_size:, :]
    return jnp.concatenate(
        [
            first_half * cosine_table - second_half * sine_table,
            second_half * cosine_table + first_half * sine_table,
        ],
        axis=-2,
    )


def attend_update(state_now, queries_blk, query_pos, keys_blk, values_blk, key_pos):
    running_max, running_sum, accumulated = state_now
    scale_value = queries_blk.shape[-1] ** (-0.5)
    scores = (
        jnp.einsum("rkgd,kdn->kgrn", queries_blk, keys_blk, preferred_element_type=jnp.float32)
        * scale_value
    )
    allowed = query_pos[:, None] >= key_pos[None, :]
    scores = jnp.where(allowed, scores, -jnp.inf)
    new_max = jnp.maximum(running_max, jnp.max(scores, axis=-1))
    weights = jnp.exp(scores - new_max[..., None])
    running_sum = jnp.sum(weights, axis=-1)
    mixed_rows = jnp.einsum(
        "kgrn,kdn->kgrd",
        weights.astype(jnp.bfloat16),
        values_blk,
        preferred_element_type=jnp.float32,
    )
    accumulated = mixed_rows
    return (new_max, running_sum, accumulated)


def keep_state(state_now):
    return state_now


def fold_step(states, fragment, first_index, groups):
    key_tile, value_tile = fragment
    key_pos = jnp.arange(key_tile.shape[2], dtype=jnp.int32)
    updated = []
    for group_entry, state_now in zip(groups, states):
        group_queries, group_first = group_entry
        row_count = group_queries.shape[0]
        query_pos = group_first + jnp.arange(row_count, dtype=jnp.int32)
        runner = partial(
            attend_update,
            queries_blk=group_queries,
            query_pos=query_pos,
            keys_blk=key_tile,
            values_blk=value_tile,
            key_pos=key_pos,
        )
        updated.append(
            lax.cond(first_index <= group_first + row_count - 1, runner, keep_state, state_now)
        )
    return tuple(updated)


def initial_state(kv_count, group_size, row_count):
    return (
        jnp.full((kv_count, group_size, row_count), -1e30, jnp.float32),
        jnp.zeros((kv_count, group_size, row_count), jnp.float32),
        jnp.zeros((kv_count, group_size, row_count, HEAD), jnp.float32),
    )


def finish_state(state_now):
    final_max, final_sum, final_acc = state_now
    result = final_acc / final_sum[..., None]
    return jnp.transpose(result, (2, 0, 1, 3)).reshape(result.shape[2], -1).astype(jnp.bfloat16)


def body(
    patches,
    patch_gain,
    patch_shift,
    encoder_up,
    encoder_down,
    proj_weight,
    hidden_text,
    slot_source,
    norm_gain,
    kv_weight,
    queries,
):
    normed_patches = layer_norm(patches, patch_gain, patch_shift)
    enc_hidden = jax.nn.gelu(
        jnp.dot(normed_patches, encoder_up, preferred_element_type=jnp.float32), approximate=False
    ).astype(jnp.bfloat16)
    partial_out = jnp.dot(enc_hidden, encoder_down, preferred_element_type=jnp.float32)
    summed_out = lax.psum(partial_out, "tp")
    encoded = (patches.astype(jnp.float32) + summed_out).astype(jnp.bfloat16)
    image_emb = jnp.dot(encoded, proj_weight, preferred_element_type=jnp.float32).astype(
        jnp.bfloat16
    )
    slot_total = slot_source.shape[0]
    slots_start = hidden_text.reshape(slot_total, PATCHES, hidden_text.shape[1])
    current = slots_start
    fragment = lax.all_gather(image_emb, "sect", axis=0, tiled=True)
    first_source = jnp.int32(0) // PATCHES
    for offset in range(fragment.shape[0] // PATCHES):
        chosen = (slot_source == first_source + offset)[:, None, None]
        current = jnp.where(
            chosen, fragment[offset * PATCHES : (offset + 1) * PATCHES][None], current
        )
    merged = current.reshape(hidden_text.shape)
    widened = merged.astype(jnp.float32)
    square_sums = lax.psum(jnp.sum(jnp.square(widened), axis=1), "tp")
    inverse = lax.rsqrt(square_sums / D + 1e-05)
    normed_hidden = (widened * inverse[:, None] * norm_gain[None, :]).astype(jnp.bfloat16)
    head_rows = kv_weight.shape[0] // lax.axis_size("tp")
    projected = lax.psum_scatter(
        lax.dot_general(
            kv_weight, normed_hidden, (((1,), (1,)), ((), ())), preferred_element_type=jnp.float32
        ),
        "tp",
        scatter_dimension=0,
        tiled=True,
    )
    row_total = queries.shape[0]
    kv_count = head_rows // (2 * HEAD)
    projected = projected.reshape(kv_count, 2, HEAD, row_total)
    block_number = lax.axis_index(("sect", "ctx"))
    first_position = block_number * row_total
    positions = (first_position + jnp.arange(row_total, dtype=jnp.int32)).astype(jnp.float32)
    rotated = rotate_keys(projected[:, 0], positions).astype(jnp.bfloat16)
    value_rows = projected[:, 1].astype(jnp.bfloat16)
    group_size = Q_HEADS // KV_HEADS
    grouped_queries = queries.reshape(row_total, kv_count, group_size, HEAD)
    groups = ((grouped_queries, first_position),)
    initial = tuple(
        [initial_state(kv_count, group_size, group_entry[0].shape[0]) for group_entry in groups]
    )
    folder = partial(fold_step, groups=groups)
    finals = folder(
        initial,
        (
            lax.all_gather(rotated, ("sect", "ctx"), axis=2, tiled=True),
            lax.all_gather(value_rows, ("sect", "ctx"), axis=2, tiled=True),
        ),
        jnp.int32(0),
    )
    results = [finish_state(state_now) for state_now in finals]
    return results[0]


def solution(mesh):
    in_specs = (
        P(("sect", "ctx"), None),
        P(),
        P(),
        P(None, "tp"),
        P("tp", None),
        P(None, "tp"),
        P(("sect", "ctx"), "tp"),
        P(("sect", "ctx")),
        P("tp"),
        P(None, "tp"),
        P(("sect", "ctx"), "tp"),
    )
    out_specs = P(("sect", "ctx"), "tp")
    return jax.shard_map(body, mesh=mesh, in_specs=in_specs, out_specs=out_specs, check_vma=False)
```

profile of v0, /device:TPU:8, one launch (start us, length us, event | category | flops | bytes accessed | tf_op | source)
XLA Modules:
  0.0 383.6 jit_solution(16793101043001423742)
XLA Ops:
  6.5 0.0 copy-start
  6.5 0.0 all-reduce.2.cloned.1.call-start
  6.5 1.2 convert_reduce_fusion
  7.8 1.2 fusion.24
  9.0 0.0 copy-start.2
  9.0 4.4 %fusion.55 = f32[128,1280]{1,0:T(8,128)} fusion(bf16[640,1280]{1,0:T(8,128)(2,1)} %param.17, bf16[1280,640]{1,0:T(8,128)(2,1)} %param.16, bf16[128,1280]{1,0:T(8,128)(2,1)} %param.13, f32[1280]{0:T(1024)} %param.15, f32[1280]{0:T(1024)} %param.14, f32[128]{0:T(128)S(1)} %add_rsqrt_fusion.1, f32[128]{0:T(128)S(1)} %broadcast_multiply_fusion), kind=kOutput, calls=%fused_computation.67 | convolution fusion | flops 425738240 | bytes 4271104 | tf_op jit(solution)/shard_map/dot_general | solution.py:122
  13.4 0.0 copy-start.4
  13.4 0.0 copy-start.3
  13.4 0.0 all-reduce.2.cloned.1.call-update
  13.5 0.0 copy-start.6
  13.5 0.0 all-gather.5.cloned.1.call-start
  13.5 69.3 %all-reduce.2.cloned.1.call-done = f32[128,1280]{1,0:T(8,128)} async-done(((f32[128,1280]{1,0:T(8,128)}), f32[128,1280]{1,0:T(8,128)}) %all-reduce.2.cloned.1.call-update) | async-done | bytes 655376 | tf_op jit(solution)/shard_map/psum | solution.py:123
  82.8 0.0 copy-done
  82.8 0.0 copy-done.2
  82.9 2.3 convolution_convert_fusion
  85.2 0.0 all-gather.5.cloned.1.call-update
  85.2 0.0 reduce-scatter.2.cloned.1.call-start
  85.2 0.0 copy-done.4
  85.3 0.1 broadcast_bitcast_fusion.2
  85.3 0.1 broadcast_bitcast_fusion
  85.4 34.6 %all-gather.5.cloned.1.call-done = bf16[512,1024]{1,0:T(8,128)(2,1)} async-done(((bf16[128,1024]{1,0:T(8,128)(2,1)}), bf16[512,1024]{1,0:T(8,128)(2,1)}) %all-gather.5.cloned.1.call-update) | async-done | bytes 1048592 | tf_op jit(solution)/shard_map/all_gather | solution.py:131
  120.0 1.3 fusion.127
  121.3 0.0 copy-done.3
  121.3 1.6 fusion.19
  122.8 14.3 %psum.15 = f32[256]{0:T(256)S(1)} all-reduce(f32[256]{0:T(256)S(1)} %get-tuple-element.38), channel_id=1, replica_groups=mesh['sect'=4,'ctx'=8,'tp'=8] {'tp'}, use_global_device_ids=true, to_apply=%region_4.5 | all-reduce | flops 256 | bytes 2048 | tf_op jit(solution)/shard_map/psum | solution.py:140
  137.2 0.0 copy-done.6
  137.2 0.0 copy-start.5
  137.2 5.1 %convolution_bitcast_fusion = f32[2048,256]{0,1:T(8,128)} fusion(bf16[2048,1024]{1,0:T(8,128)(2,1)} %param.22, bf16[256,1024]{1,0:T(8,128)(2,1)} %get-tuple-element.39, f32[1024]{0:T(1024)S(1)} %copy-done.6, f32[256]{0:T(256)S(1)} %add_rsqrt_fusion), kind=kOutput, calls=%fused_computation.19 | convolution fusion | flops 1074790400 | bytes 6820864 | tf_op jit(solution)/shard_map/dot_general | solution.py:145
  142.3 0.0 reduce-scatter.2.cloned.1.call-update
  142.3 0.0 all-gather.7.cloned.1.call-start
  142.4 31.3 %reduce-scatter.2.cloned.1.call-done = f32[256,256]{0,1:T(8,128)} async-done(((f32[2048,256]{0,1:T(8,128)}), f32[256,256]{0,1:T(8,128)}) %reduce-scatter.2.cloned.1.call-update) | async-done | bytes 262160 | tf_op jit(solution)/shard_map/reduce_scatter | solution.py:144
  173.7 1.1 copy.20
  174.8 0.3 fusion.93
  175.1 0.6 pad_maximum_fusion
  175.7 0.0 all-gather.7.cloned.1.call-update
  175.8 0.2 all-gather.9.cloned.1.call-start
  176.0 0.6 slice.47
  176.6 0.0 all-gather.9.cloned.1.call-update
  176.6 73.0 %all-gather.7.cloned.1.call-done = bf16[1,128,8192]{2,1,0:T(8,128)(2,1)} async-done(((bf16[1,128,256]{2,1,0:T(8,128)(2,1)}), bf16[1,128,8192]{2,1,0:T(8,128)(2,1)}) %all-gather.7.cloned.1.call-update) | async-done | bytes 2097168 | tf_op jit(solution)/shard_map/all_gather | solution.py:170
  249.6 76.4 %all-gather.9.cloned.1.call-done = bf16[1,1,128,8192]{3,2,1,0:T(8,128)(2,1)} async-done(((bf16[1,1,128,256]{3,2,1,0:T(8,128)(2,1)}), bf16[1,1,128,8192]{3,2,1,0:T(8,128)(2,1)}) %all-gather.9.cloned.1.call-update) | async-done | bytes 2097168 | tf_op jit(solution)/shard_map/all_gather | solution.py:171
  326.1 0.0 copy-done.5
  326.1 49.8 %conditional.1 = (f32[1,4,256]{2,1,0:T(4,128)S(1)}, f32[1,4,256,128]{3,2,1,0:T(8,128)S(1)}) conditional(s32[]{:T(128)} %convert_element_type.65, () %tuple.13, (s32[]{:T(128)}, s32[256]{0:T(256)S(1)}, s32[8192]{0:T(1024)S(1)}, bf16[1,128,8192]{2,1,0:T(8,128)(2,1)}, bf16[256,512]{1,0:T(8,128)(2,1)S(1)}, ...), branch_computations={%region_6.7_spmd, %region_7.10_spmd} | conditional | flops 4389338112 | bytes 122481712 | solution.py:86
  326.1 3.7 broadcast_compare_fusion
  329.8 0.0 copy-start.1
  329.8 15.6 %fusion.2 = (f32[4,256]{1,0:T(4,128)S(1)}, f32[8192,256,4]{1,0,2:T(8,128)}) fusion(pred[256,8192]{0,1:T(8,128)(4,1)S(1)} %broadcast_compare_fusion, bf16[1,128,8192]{2,1,0:T(8,128)(2,1)} %get-tuple-element.35, bf16[256,512]{1,0:T(8,128)(2,1)S(1)} %get-tuple-element.31), kind=kOutput, calls=%fused_computation.4 | convolution fusion | flops 2172648448 | bytes 38014976 | tf_op jit(solution)/shard_map/cond/branch_1_fun/rkgd,kdn->kgrn/dot_general | solution.py:47
  345.5 0.0 copy-done.1
  345.5 15.8 %fusion.10 = f32[1,4,256,128]{3,2,1,0:T(8,128)S(1)} fusion(bf16[1,128,8192]{2,1,0:T(8,128)(2,1)} %get-tuple-element.25, f32[8192,256,4]{1,0,2:T(8,128)} %get-tuple-element.41, f32[4,256]{1,0:T(4,128)S(1)} %broadcast_maximum_fusion, pred[256,8192]{0,1:T(8,128)(4,1)} %copy-done.1), kind=kOutput, calls=%fused_computation.12 | convolution fusion | flops 2181038080 | bytes 38277120 | tf_op jit(solution)/shard_map/cond/branch_1_fun/kgrn,kdn->kgrd/dot_general | solution.py:55
  361.2 14.6 %fusion.1 = f32[4,256]{1,0:T(4,128)S(1)} fusion(f32[8192,256,4]{1,0,2:T(8,128)} %get-tuple-element.41, f32[4,256]{1,0:T(4,128)S(1)} %broadcast_maximum_fusion, pred[256,8192]{0,1:T(8,128)(4,1)} %copy-done.1), kind=kLoop, calls=%fused_computation.3 | loop fusion | flops 33553408 | bytes 35659776 | tf_op jit(solution)/shard_map/cond/branch_1_fun/reduce_sum | solution.py:54
  375.9 0.2 fusion.57
  376.1 0.2 copy.22
  376.3 0.7 copy.33
  (11 shorter events, 0.1 us)
Async XLA Ops:
  6.5 76.3 %copy-start = (bf16[1280,1024]{1,0:T(8,128)(2,1)S(1)}, bf16[1280,1024]{1,0:T(8,128)(2,1)}, u32[]{:S(2)}) copy-start(bf16[1280,1024]{1,0:T(8,128)(2,1)} %param.18) | copy-start | bytes 7864324
  6.5 76.3 %all-reduce.2.cloned.1.call-start = ((), (), s32[]{:S(2)}) async-start(), calls=%async_computation.1 | async-start | bytes 1310720 | tf_op jit(solution)/shard_map/psum | solution.py:123
  9.0 73.8 %copy-start.2 = (bf16[128,1280]{1,0:T(8,128)(2,1)S(1)}, bf16[128,1280]{1,0:T(8,128)(2,1)}, u32[]{:S(2)}) copy-start(bf16[128,1280]{1,0:T(8,128)(2,1)} %param.13) | copy-start | bytes 983044
  13.4 71.8 %copy-start.4 = (s32[2]{0:T(128)S(1)}, s32[2]{0:T(128)}, u32[]{:S(2)}) copy-start(s32[2]{0:T(128)} %param.20) | copy-start | bytes 28
  13.4 107.8 %copy-start.3 = (bf16[256,1024]{1,0:T(8,128)(2,1)S(1)}, bf16[256,1024]{1,0:T(8,128)(2,1)}, u32[]{:S(2)}) copy-start(bf16[256,1024]{1,0:T(8,128)(2,1)} %param.19) | copy-start | bytes 1572868
  13.5 123.7 %copy-start.6 = (f32[1024]{0:T(1024)S(1)}, f32[1024]{0:T(1024)}, u32[]{:S(2)}) copy-start(f32[1024]{0:T(1024)} %param.21) | copy-start | bytes 12292
  13.5 106.5 %all-gather.5.cloned.1.call-start = ((), (), s32[]{:S(2)}) async-start(), calls=%async_computation.2 | async-start | bytes 1310720 | tf_op jit(solution)/shard_map/all_gather | solution.py:131
  85.2 88.5 %reduce-scatter.2.cloned.1.call-start = ((), (), s32[]{:S(2)}) async-start(), calls=%async_computation.3 | async-start | bytes 2359296 | tf_op jit(solution)/shard_map/reduce_scatter | solution.py:144
  137.2 188.9 %copy-start.5 = (bf16[256,512]{1,0:T(8,128)(2,1)S(1)}, bf16[256,512]{1,0:T(8,128)(2,1)}, u32[]{:S(2)}) copy-start(bf16[256,512]{1,0:T(8,128)(2,1)} %param.23) | copy-start | bytes 786436
  142.3 107.3 %all-gather.7.cloned.1.call-start = ((), (), s32[]{:S(2)}) async-start(), calls=%async_computation.4 | async-start | bytes 2162688 | tf_op jit(solution)/shard_map/all_gather | solution.py:170
  175.8 150.3 %all-gather.9.cloned.1.call-start = ((), (), s32[]{:S(2)}) async-start(), calls=%async_computation.5 | async-start | bytes 2162688 | tf_op jit(solution)/shard_map/all_gather | solution.py:171
  329.8 15.6 %copy-start.1 = (pred[256,8192]{0,1:T(8,128)(4,1)}, pred[256,8192]{0,1:T(8,128)(4,1)S(1)}, u32[]{:S(2)}) copy-start(pred[256,8192]{0,1:T(8,128)(4,1)S(1)} %broadcast_compare_fusion) | copy-start | bytes 6291460 | tf_op jit(solution)/shard_map/cond
Sparse Core Ops, SparseCore 0:
  13.6 69.2 all-reduce.1
  85.3 34.6 all-gather.4
  142.4 31.1 reduce-scatter.1
  176.0 73.6 all-gather.6
  252.0 74.0 all-gather.8
where the time goes:
time: 384 us
  waiting for transfers between devices  285 us (74%)
  matrix products  43.2 us (11%)
  other arithmetic  23.6 us (6%)
  blocking collectives  14.3 us (4%)
  between operations  13.3 us (3%)
  local copies, waits for them, and re-layouts  4.12 us (1%)
    all_gather x1, waiting for transfers between devices, body(): lax.all_gather(value_rows, ('sect', 'ctx'), axis=2, tiled=True)  76.4 us
    all_gather x1, waiting for transfers between devices, body(): lax.all_gather(rotated, ('sect', 'ctx'), axis=2, tiled=True)  73 us
    psum x1, waiting for transfers between devices, body(): summed_out = lax.psum(partial_out, 'tp')  69.3 us
    all_gather x1, waiting for transfers between devices, body(): fragment = lax.all_gather(image_emb, 'sect', axis=0, tiled=True)  34.6 us
    reduce_scatter x1, waiting for transfers between devices, body(): lax.psum_scatter(lax.dot_general(kv_weight, normed_hidden, (((1,), (1,)),...  31.3 us
    dot_general x1, matrix products, attend_update(): jnp.einsum('kgrn,kdn->kgrd', weights.astype(jnp.bfloat16), values_blk, pr...  15.8 us
    dot_general x1, matrix products, attend_update(): jnp.einsum('rkgd,kdn->kgrn', queries_blk, keys_blk, preferred_element_typ...  15.6 us
    reduce_sum x1, other arithmetic, attend_update(): running_sum = jnp.sum(weights, axis=-1)  14.6 us
  transfers between devices with their start and end apart: 5, of which 5 were waited for; matrix products, arithmetic and copies ran while one was open for 0% of the time, Pallas kernels for 0%

commit v1 on v0

--- a/solution.py
+++ b/solution.py
@@ -137,7 +137,7 @@
         )
     merged = current.reshape(hidden_text.shape)
     widened = merged.astype(jnp.float32)
-    square_sums = lax.psum(jnp.sum(jnp.square(widened), axis=1), "tp")
+    square_sums = jnp.sum(lax.all_gather(jnp.sum(jnp.square(widened), axis=1), "tp"), axis=0)
     inverse = lax.rsqrt(square_sums / D + 1e-05)
     normed_hidden = (widened * inverse[:, None] * norm_gain[None, :]).astype(jnp.bfloat16)
     head_rows = kv_weight.shape[0] // lax.axis_size("tp")

time: 384 us -> 381 us (level)
    psum x1 -> x0, blocking collectives: 14.3 us -> none  [body(): square_sums = lax.psum(jnp.sum(jnp.square(widened), axis=1), 'tp')]
    all_gather x0 -> x1, blocking collectives: none -> 10.5 us  [body(): lax.all_gather(jnp.sum(jnp.square(widened), axis=1), 'tp')]
where the time goes in v1:
time: 381 us; the launch traced here: 380 us
  waiting for transfers between devices  285 us (75%)
  matrix products  43.2 us (11%)
  other arithmetic  23.7 us (6%)
  between operations  13.3 us (3%)
  blocking collectives  10.5 us (3%)
  local copies, waits for them, and re-layouts  4.13 us (1%)
    all_gather x1, waiting for transfers between devices, body(): lax.all_gather(value_rows, ('sect', 'ctx'), axis=2, tiled=True)  76.4 us
    all_gather x1, waiting for transfers between devices, body(): lax.all_gather(rotated, ('sect', 'ctx'), axis=2, tiled=True)  73.2 us
    psum x1, waiting for transfers between devices, body(): summed_out = lax.psum(partial_out, 'tp')  69.3 us
    all_gather x1, waiting for transfers between devices, body(): fragment = lax.all_gather(image_emb, 'sect', axis=0, tiled=True)  34.6 us
    reduce_scatter x1, waiting for transfers between devices, body(): lax.psum_scatter(lax.dot_general(kv_weight, normed_hidden, (((1,), (1,)),...  31.6 us
    dot_general x1, matrix products, attend_update(): jnp.einsum('kgrn,kdn->kgrd', weights.astype(jnp.bfloat16), values_blk, pr...  15.8 us
    dot_general x1, matrix products, attend_update(): jnp.einsum('rkgd,kdn->kgrn', queries_blk, keys_blk, preferred_element_typ...  15.6 us
    reduce_sum x1, other arithmetic, attend_update(): running_sum = jnp.sum(weights, axis=-1)  14.6 us
  transfers between devices with their start and end apart: 5, of which 5 were waited for; matrix products, arithmetic and copies ran while one was open for 0% of the time, Pallas kernels for 0%

profile of v1, /device:TPU:8, one launch (start us, length us, event | category | flops | bytes accessed | tf_op | source)
XLA Modules:
  0.0 380.3 jit_solution(5974026323606674378)
XLA Ops:
  6.5 0.0 copy-start
  6.5 0.0 all-reduce.2.cloned.1.call-start
  6.5 1.2 convert_reduce_fusion
  7.8 1.2 fusion.24
  9.0 0.0 copy-start.2
  9.0 4.4 %fusion.55 = f32[128,1280]{1,0:T(8,128)} fusion(bf16[640,1280]{1,0:T(8,128)(2,1)} %param.17, bf16[1280,640]{1,0:T(8,128)(2,1)} %param.16, bf16[128,1280]{1,0:T(8,128)(2,1)} %param.13, f32[1280]{0:T(1024)} %param.15, f32[1280]{0:T(1024)} %param.14, f32[128]{0:T(128)S(1)} %add_rsqrt_fusion.1, f32[128]{0:T(128)S(1)} %broadcast_multiply_fusion), kind=kOutput, calls=%fused_computation.67 | convolution fusion | flops 425738240 | bytes 4271104 | tf_op jit(solution)/shard_map/dot_general | solution.py:122
  13.4 0.0 copy-start.4
  13.4 0.0 copy-start.3
  13.4 0.0 all-reduce.2.cloned.1.call-update
  13.5 0.0 copy-start.6
  13.5 0.0 all-gather.7.cloned.1.call-start
  13.5 69.3 %all-reduce.2.cloned.1.call-done = f32[128,1280]{1,0:T(8,128)} async-done(((f32[128,1280]{1,0:T(8,128)}), f32[128,1280]{1,0:T(8,128)}) %all-reduce.2.cloned.1.call-update) | async-done | bytes 655376 | tf_op jit(solution)/shard_map/psum | solution.py:123
  82.8 0.0 copy-done
  82.8 0.0 copy-done.2
  82.9 2.3 convolution_convert_fusion
  85.2 0.0 all-gather.7.cloned.1.call-update
  85.2 0.0 reduce-scatter.2.cloned.1.call-start
  85.2 0.0 copy-done.4
  85.3 0.1 broadcast_bitcast_fusion.2
  85.3 0.1 broadcast_bitcast_fusion
  85.4 34.6 %all-gather.7.cloned.1.call-done = bf16[512,1024]{1,0:T(8,128)(2,1)} async-done(((bf16[128,1024]{1,0:T(8,128)(2,1)}), bf16[512,1024]{1,0:T(8,128)(2,1)}) %all-gather.7.cloned.1.call-update) | async-done | bytes 1048592 | tf_op jit(solution)/shard_map/all_gather | solution.py:131
  120.0 1.3 fusion.127
  121.3 0.0 copy-done.3
  121.3 1.6 fusion.19
  122.8 10.5 %all-gather.2 = f32[8,1,256]{2,1,0:T(1,128)S(1)} all-gather(f32[1,1,256]{2,1,0:T(1,128)S(1)} %bitcast.96), channel_id=2, replica_groups=mesh['sect'=4,'ctx'=8,'tp'=8] {'tp'}, dimensions={0}, use_global_device_ids=true | all-gather | bytes 9216 | tf_op jit(solution)/shard_map/all_gather | solution.py:140
  133.4 0.0 copy-done.6
  133.4 0.0 copy-start.5
  133.4 5.1 %convolution_bitcast_fusion = f32[2048,256]{0,1:T(8,128)} fusion(bf16[2048,1024]{1,0:T(8,128)(2,1)} %param.22, bf16[256,1024]{1,0:T(8,128)(2,1)} %get-tuple-element.39, f32[1024]{0:T(1024)S(1)} %copy-done.6, f32[256]{0:T(256)S(1)} %add_rsqrt_fusion), kind=kOutput, calls=%fused_computation.19 | convolution fusion | flops 1074790400 | bytes 6820864 | tf_op jit(solution)/shard_map/dot_general | solution.py:145
  138.4 0.0 reduce-scatter.2.cloned.1.call-update
  138.5 0.0 all-gather.9.cloned.1.call-start
  138.6 31.6 %reduce-scatter.2.cloned.1.call-done = f32[256,256]{0,1:T(8,128)} async-done(((f32[2048,256]{0,1:T(8,128)}), f32[256,256]{0,1:T(8,128)}) %reduce-scatter.2.cloned.1.call-update) | async-done | bytes 262160 | tf_op jit(solution)/shard_map/reduce_scatter | solution.py:144
  170.2 1.1 copy.25
  171.3 0.3 fusion.93
  171.6 0.6 pad_maximum_fusion
  172.2 0.0 all-gather.9.cloned.1.call-update
  172.3 0.2 all-gather.11.cloned.1.call-start
  172.5 0.6 slice.47
  173.1 0.0 all-gather.11.cloned.1.call-update
  173.1 73.2 %all-gather.9.cloned.1.call-done = bf16[1,128,8192]{2,1,0:T(8,128)(2,1)} async-done(((bf16[1,128,256]{2,1,0:T(8,128)(2,1)}), bf16[1,128,8192]{2,1,0:T(8,128)(2,1)}) %all-gather.9.cloned.1.call-update) | async-done | bytes 2097168 | tf_op jit(solution)/shard_map/all_gather | solution.py:170
  246.3 76.4 %all-gather.11.cloned.1.call-done = bf16[1,1,128,8192]{3,2,1,0:T(8,128)(2,1)} async-done(((bf16[1,1,128,256]{3,2,1,0:T(8,128)(2,1)}), bf16[1,1,128,8192]{3,2,1,0:T(8,128)(2,1)}) %all-gather.11.cloned.1.call-update) | async-done | bytes 2097168 | tf_op jit(solution)/shard_map/all_gather | solution.py:171
  322.7 0.0 copy-done.5
  322.7 49.8 %conditional.1 = (f32[1,4,256]{2,1,0:T(4,128)S(1)}, f32[1,4,256,128]{3,2,1,0:T(8,128)S(1)}) conditional(s32[]{:T(128)} %convert_element_type.65, () %tuple.13, (s32[]{:T(128)}, s32[256]{0:T(256)S(1)}, s32[8192]{0:T(1024)S(1)}, bf16[1,128,8192]{2,1,0:T(8,128)(2,1)}, bf16[256,512]{1,0:T(8,128)(2,1)S(1)}, ...), branch_computations={%region_6.7_spmd, %region_7.10_spmd} | conditional | flops 4389338112 | bytes 122481712 | solution.py:86
  322.7 3.7 broadcast_compare_fusion
  326.5 0.0 copy-start.1
  326.5 15.6 %fusion.2 = (f32[4,256]{1,0:T(4,128)S(1)}, f32[8192,256,4]{1,0,2:T(8,128)}) fusion(pred[256,8192]{0,1:T(8,128)(4,1)S(1)} %broadcast_compare_fusion, bf16[1,128,8192]{2,1,0:T(8,128)(2,1)} %get-tuple-element.35, bf16[256,512]{1,0:T(8,128)(2,1)S(1)} %get-tuple-element.31), kind=kOutput, calls=%fused_computation.4 | convolution fusion | flops 2172648448 | bytes 38014976 | tf_op jit(solution)/shard_map/cond/branch_1_fun/rkgd,kdn->kgrn/dot_general | solution.py:47
  342.1 0.0 copy-done.1
  342.1 15.8 %fusion.10 = f32[1,4,256,128]{3,2,1,0:T(8,128)S(1)} fusion(bf16[1,128,8192]{2,1,0:T(8,128)(2,1)} %get-tuple-element.25, f32[8192,256,4]{1,0,2:T(8,128)} %get-tuple-element.41, f32[4,256]{1,0:T(4,128)S(1)} %broadcast_maximum_fusion, pred[256,8192]{0,1:T(8,128)(4,1)} %copy-done.1), kind=kOutput, calls=%fused_computation.12 | convolution fusion | flops 2181038080 | bytes 38277120 | tf_op jit(solution)/shard_map/cond/branch_1_fun/kgrn,kdn->kgrd/dot_general | solution.py:55
  357.9 14.6 %fusion.1 = f32[4,256]{1,0:T(4,128)S(1)} fusion(f32[8192,256,4]{1,0,2:T(8,128)} %get-tuple-element.41, f32[4,256]{1,0:T(4,128)S(1)} %broadcast_maximum_fusion, pred[256,8192]{0,1:T(8,128)(4,1)} %copy-done.1), kind=kLoop, calls=%fused_computation.3 | loop fusion | flops 33553408 | bytes 35659776 | tf_op jit(solution)/shard_map/cond/branch_1_fun/reduce_sum | solution.py:54
  372.6 0.2 fusion.57
  372.8 0.2 copy.27
  373.0 0.7 copy.38
  (12 shorter events, 0.1 us)
Async XLA Ops:
  6.5 76.3 %copy-start = (bf16[1280,1024]{1,0:T(8,128)(2,1)S(1)}, bf16[1280,1024]{1,0:T(8,128)(2,1)}, u32[]{:S(2)}) copy-start(bf16[1280,1024]{1,0:T(8,128)(2,1)} %param.18) | copy-start | bytes 7864324
  6.5 76.3 %all-reduce.2.cloned.1.call-start = ((), (), s32[]{:S(2)}) async-start(), calls=%async_computation.1 | async-start | bytes 1310720 | tf_op jit(solution)/shard_map/psum | solution.py:123
  9.0 73.8 %copy-start.2 = (bf16[128,1280]{1,0:T(8,128)(2,1)S(1)}, bf16[128,1280]{1,0:T(8,128)(2,1)}, u32[]{:S(2)}) copy-start(bf16[128,1280]{1,0:T(8,128)(2,1)} %param.13) | copy-start | bytes 983044
  13.4 71.8 %copy-start.4 = (s32[2]{0:T(128)S(1)}, s32[2]{0:T(128)}, u32[]{:S(2)}) copy-start(s32[2]{0:T(128)} %param.20) | copy-start | bytes 28
  13.4 107.8 %copy-start.3 = (bf16[256,1024]{1,0:T(8,128)(2,1)S(1)}, bf16[256,1024]{1,0:T(8,128)(2,1)}, u32[]{:S(2)}) copy-start(bf16[256,1024]{1,0:T(8,128)(2,1)} %param.19) | copy-start | bytes 1572868
  13.5 119.9 %copy-start.6 = (f32[1024]{0:T(1024)S(1)}, f32[1024]{0:T(1024)}, u32[]{:S(2)}) copy-start(f32[1024]{0:T(1024)} %param.21) | copy-start | bytes 12292
  13.5 106.5 %all-gather.7.cloned.1.call-start = ((), (), s32[]{:S(2)}) async-start(), calls=%async_computation.2 | async-start | bytes 1310720 | tf_op jit(solution)/shard_map/all_gather | solution.py:131
  85.2 85.0 %reduce-scatter.2.cloned.1.call-start = ((), (), s32[]{:S(2)}) async-start(), calls=%async_computation.3 | async-start | bytes 2359296 | tf_op jit(solution)/shard_map/reduce_scatter | solution.py:144
  133.4 189.4 %copy-start.5 = (bf16[256,512]{1,0:T(8,128)(2,1)S(1)}, bf16[256,512]{1,0:T(8,128)(2,1)}, u32[]{:S(2)}) copy-start(bf16[256,512]{1,0:T(8,128)(2,1)} %param.23) | copy-start | bytes 786436
  138.5 107.8 %all-gather.9.cloned.1.call-start = ((), (), s32[]{:S(2)}) async-start(), calls=%async_computation.4 | async-start | bytes 2162688 | tf_op jit(solution)/shard_map/all_gather | solution.py:170
  172.3 150.4 %all-gather.11.cloned.1.call-start = ((), (), s32[]{:S(2)}) async-start(), calls=%async_computation.5 | async-start | bytes 2162688 | tf_op jit(solution)/shard_map/all_gather | solution.py:171
  326.5 15.6 %copy-start.1 = (pred[256,8192]{0,1:T(8,128)(4,1)}, pred[256,8192]{0,1:T(8,128)(4,1)S(1)}, u32[]{:S(2)}) copy-start(pred[256,8192]{0,1:T(8,128)(4,1)S(1)} %broadcast_compare_fusion) | copy-start | bytes 6291460 | tf_op jit(solution)/shard_map/cond
Sparse Core Ops, SparseCore 0:
  13.6 69.2 all-reduce.1
  85.3 34.6 all-gather.6
  138.6 31.5 reduce-scatter.1
  172.5 73.7 all-gather.8
  248.6 74.0 all-gather.10
